TPU v7x, 128 devices: a whole 4x4x4 slice. The times are simulated.
128 devices in a mesh: ctx: 8 (over y, core), uly: 16 (over z, x).
Axes of the slice: x: 4, y: 4, z: 4, core: 2. Of those that a mesh axis runs over, the one named last changes fastest.
Arguments:
- queries: bfloat16 [131072, 2048], P(('ctx', 'uly')), may hold values from -6 to 6
- key_vectors: bfloat16 [131072, 2048], P(('ctx', 'uly')), may hold values from -0.52734375 to 0.52734375
- value_vectors: bfloat16 [131072, 2048], P(('ctx', 'uly')), may hold values from -6 to 6
- level_gates: bfloat16 [131072, 192], P(('ctx', 'uly')), may hold values from 0.049804688 to 1
Outputs:
- attended: bfloat16 [131072, 2048], P(('ctx', 'uly'))
All inputs are finite; a program needn't handle non-finite values.
Results may differ from a plain program's by a relative error of at most 0.005.
Values may be sent and summed in bfloat16 or wider, within the bound.
A program may use at most 192 MiB of HBM per device.

v0:
```python
import jax
import jax.numpy as jnp
from jax import lax
from jax.sharding import PartitionSpec as P

HEAD_DIM = 128
BLOCK = 64


def level_scale(level_no):
    return (BLOCK * 2 ** max(level_no - 1, 0)) ** (-0.5)


def head_levels(query_rows, key_rows, value_rows, head_weight):
    row_total = query_rows.shape[0]
    block_total = row_total // BLOCK
    query_blocks = query_rows.reshape(block_total, BLOCK, HEAD_DIM)
    key_blocks = key_rows.reshape(block_total, BLOCK, HEAD_DIM)
    value_blocks = value_rows.reshape(block_total, BLOCK, HEAD_DIM)
    causal = jnp.tril(jnp.ones((BLOCK, BLOCK), dtype=bool))
    scores = jnp.einsum(
        "cid,cjd->cij", query_blocks, key_blocks, preferred_element_type=jnp.float32
    )
    scores = jnp.where(causal[None], scores, 0.0).astype(jnp.bfloat16)
    output = jnp.einsum("cij,cjd->cid", scores, value_blocks, preferred_element_type=jnp.float32)
    output = output.reshape(row_total, HEAD_DIM) * (head_weight[0] * level_scale(0))[:, None]
    current = jnp.einsum(
        "cid,cie->cde", key_blocks, value_blocks, preferred_element_type=jnp.float32
    )
    positions = jnp.arange(row_total, dtype=jnp.int32)
    level_no = 1
    span_len = BLOCK
    while span_len < row_total:
        pair_count = row_total // (2 * span_len)
        paired = current.reshape(pair_count, 2, HEAD_DIM, HEAD_DIM)
        earlier = paired[:, 0].astype(jnp.bfloat16)
        pair_queries = query_rows.reshape(pair_count, 2 * span_len, HEAD_DIM)
        partial_value = jnp.einsum(
            "bte,bef->btf", pair_queries, earlier, preferred_element_type=jnp.float32
        )
        later_half = (positions // span_len % 2).astype(jnp.float32)
        factor = head_weight[level_no] * later_half * level_scale(level_no)
        output = output + partial_value.reshape(row_total, HEAD_DIM) * factor[:, None]
        current = paired[:, 0] + paired[:, 1]
        level_no += 1
        span_len *= 2
    return (output, current[0], level_no)


def ctx_remote(totals):
    group_size = lax.axis_size("ctx")
    position = lax.axis_index("ctx")
    step_total = group_size.bit_length() - 1
    remote_states = []
    gathered = lax.all_gather(totals[None], "ctx", axis=0, tiled=True)
    member = jnp.arange(group_size, dtype=jnp.int32)
    for step_no in range(1, step_total + 1):
        selector = (member >> step_no == position >> step_no) & (member >> step_no - 1 & 1 == 0)
        selector = selector & (position >> step_no - 1 & 1 == 1)
        remote_states.append(
            jnp.sum(gathered * selector.astype(jnp.float32)[:, None, None, None], axis=0)
        )
    return remote_states


def local_pass(query_rows, key_rows, value_rows, gate_rows, head_count):
    row_total = query_rows.shape[0]
    level_total = gate_rows.shape[1] // head_count
    weight_table = jnp.transpose(
        gate_rows.astype(jnp.float32).reshape(row_total, head_count, level_total), (1, 2, 0)
    )
    first_level = 1
    head_out, head_total, first_level = head_levels(
        query_rows, key_rows, value_rows, weight_table[0]
    )
    outputs = [head_out]
    totals = [head_total]
    return (outputs, jnp.stack(totals, axis=0), first_level, weight_table)


def finish(outputs, query_rows, weight_table, remote_states, first_level):
    finished = []
    for head_no, head_out in enumerate(outputs):
        for offset, remote_state in enumerate(remote_states):
            level_no = first_level + offset
            partial_value = jnp.dot(
                query_rows,
                remote_state[head_no].astype(jnp.bfloat16),
                preferred_element_type=jnp.float32,
            )
            head_out = (
                head_out
                + partial_value * (weight_table[head_no, level_no] * level_scale(level_no))[:, None]
            )
        finished.append(head_out)
    return finished[0].astype(jnp.bfloat16)


def shards(queries, key_vectors, value_vectors, level_gates):
    moved_query, moved_key, moved_value, moved_gate = (
        lax.all_to_all(queries, "uly", split_axis=1, concat_axis=0, tiled=True),
        lax.all_to_all(key_vectors, "uly", split_axis=1, concat_axis=0, tiled=True),
        lax.all_to_all(value_vectors, "uly", split_axis=1, concat_axis=0, tiled=True),
        lax.all_to_all(level_gates, "uly", split_axis=1, concat_axis=0, tiled=True),
    )
    head_count = moved_query.shape[1] // HEAD_DIM
    outputs, totals, first_level, weight_table = local_pass(
        moved_query, moved_key, moved_value, moved_gate, head_count
    )
    result = finish(outputs, moved_query, weight_table, ctx_remote(totals), first_level)
    return lax.all_to_all(result, "uly", split_axis=0, concat_axis=1, tiled=True)


def solution(mesh):
    in_specs = (
        P(("ctx", "uly"), None),
        P(("ctx", "uly"), None),
        P(("ctx", "uly"), None),
        P(("ctx", "uly"), None),
    )
    out_specs = P(("ctx", "uly"), None)
    return jax.shard_map(shards, mesh=mesh, in_specs=in_specs, out_specs=out_specs, check_vma=False)
```

profile of v0, /device:TPU:0, one launch (start us, length us, event | category | flops | bytes accessed | tf_op | source)
XLA Modules:
  0.0 558.2 jit_solution(340327055018830917)
XLA Ops:
  0.0 1.9 all_to_all.69
  1.9 8.0 %all-to-all-start.3 = ((bf16[1024,16,12]{0,2,1:T(8,128)(2,1)}), bf16[1024,16,12]{0,2,1:T(8,128)(2,1)S(1)}, u32[]{:S(2)}, u32[]{:S(2)}) async-start(bf16[1024,16,12]{0,2,1:T(8,128)(2,1)} %all_to_all.69), calls=%async_computation.3 | async-start | bytes 1048576 | tf_op jit(solution)/shard_map/all_to_all | solution.py:104
  9.9 5.3 copy_bitcast_fusion.2
  15.1 6.2 %all-to-all-done.3 = bf16[1024,16,12]{0,2,1:T(8,128)(2,1)S(1)} async-done(((bf16[1024,16,12]{0,2,1:T(8,128)(2,1)}), bf16[1024,16,12]{0,2,1:T(8,128)(2,1)S(1)}, u32[]{:S(2)}, u32[]{:S(2)}) %all-to-all-start.3) | async-done | bytes 393248 | tf_op jit(solution)/shard_map/all_to_all | solution.py:104
  21.4 4.6 all-to-all-start.1
  26.0 5.2 copy_bitcast_fusion.1
  31.2 55.1 %all-to-all-done.1 = bf16[1024,16,128]{2,0,1:T(8,128)(2,1)} async-done(((bf16[1024,16,128]{2,0,1:T(8,128)(2,1)}), bf16[1024,16,128]{2,0,1:T(8,128)(2,1)}, u32[]{:S(2)}, u32[]{:S(2)}) %all-to-all-start.1) | async-done | bytes 4194336 | tf_op jit(solution)/shard_map/all_to_all | solution.py:102
  86.3 4.6 all-to-all-start.2
  90.8 6.4 %copy.58 = bf16[1024,2048]{0,1:T(8,128)(2,1)} copy(bf16[1024,2048]{1,0:T(8,128)(2,1)} %param.4) | data formatting | bytes 8388608 | tf_op args[0]
  97.2 6.3 %copy.59 = bf16[1024,16,128]{2,0,1:T(8,128)(2,1)} copy(bf16[1024,16,128]{0,2,1:T(8,128)(2,1)} %bitcast.250) | data formatting | bytes 8388608 | tf_op jit(solution)/shard_map/all_to_all | solution.py:101
  104.4 44.0 %all-to-all-done.2 = bf16[1024,16,128]{2,0,1:T(8,128)(2,1)} async-done(((bf16[1024,16,128]{2,0,1:T(8,128)(2,1)}), bf16[1024,16,128]{2,0,1:T(8,128)(2,1)}, u32[]{:S(2)}, u32[]{:S(2)}) %all-to-all-start.2) | async-done | bytes 4194336 | tf_op jit(solution)/shard_map/all_to_all | solution.py:103
  148.4 4.7 all-to-all-start
  157.1 11.6 %fusion.103 = f32[256,128,128]{2,1,0:T(8,128)} fusion(bf16[256,64,128]{2,1,0:T(8,128)(2,1)} %bitcast.4, bf16[256,64,128]{2,1,0:T(8,128)(2,1)} %bitcast.6), kind=kOutput, calls=%fused_computation.183 | convolution fusion | flops 536870912 | bytes 25165824 | tf_op jit(solution)/shard_map/cid,cie->cde/dot_general | solution.py:27
  168.7 38.2 %all-to-all-done = bf16[1024,16,128]{2,0,1:T(8,128)(2,1)} async-done(((bf16[1024,16,128]{2,0,1:T(8,128)(2,1)}), bf16[1024,16,128]{2,0,1:T(8,128)(2,1)}, u32[]{:S(2)}, u32[]{:S(2)}) %all-to-all-start) | async-done | bytes 4194336 | tf_op jit(solution)/shard_map/all_to_all | solution.py:101
  207.0 11.4 %fusion.14 = f32[256,64,128]{2,1,0:T(8,128)} fusion(bf16[256,64,128]{2,1,0:T(8,128)(2,1)} %bitcast.6, pred[64,64]{1,0:T(8,128)(4,1)S(1)} %iota_compare_fusion, bf16[256,64,128]{2,1,0:T(8,128)(2,1)} %bitcast.2, bf16[256,64,128]{2,1,0:T(8,128)(2,1)} %bitcast.4), kind=kOutput, calls=%fused_computation.23 | convolution fusion | flops 538968064 | bytes 20975616 | tf_op jit(solution)/shard_map/cij,cjd->cid/dot_general | solution.py:25
  218.4 9.0 %copy.63 = f32[16384,128]{0,1:T(8,128)} copy(f32[16384,128]{1,0:T(8,128)} %bitcast.238) | data formatting | bytes 16777216 | tf_op jit(solution)/shard_map/reshape | solution.py:26
  227.4 11.7 %fusion.9 = f32[128,1,128,128]{3,2,0,1:T(8,128)} fusion(f32[128,2,128,128]{3,2,1,0:T(8,128)} %bitcast.235), kind=kLoop, calls=%fused_computation.15 | loop fusion | flops 2097152 | bytes 25165824 | tf_op jit(solution)/shard_map/add | solution.py:44
  239.1 9.2 %fusion.12 = f32[128,128,128]{1,2,0:T(8,128)} fusion(bf16[128,128,128]{2,1,0:T(8,128)(2,1)} %bitcast.15, f32[128,2,128,128]{3,2,1,0:T(8,128)} %bitcast.236), kind=kOutput, calls=%fused_computation.22 | convolution fusion | flops 536870912 | bytes 16777216 | tf_op jit(solution)/shard_map/bte,bef->btf/dot_general | solution.py:38
  248.3 9.0 %copy.65 = f32[16384,128]{0,1:T(8,128)} copy(f32[16384,128]{1,0:T(8,128)} %bitcast.239) | data formatting | bytes 16777216 | tf_op jit(solution)/shard_map/reshape | solution.py:43
  257.2 8.0 %fusion.102 = (f32[64,1,128,128]{3,2,1,0:T(8,128)}, f32[64,1,128,128]{3,2,1,0:T(8,128)}) fusion(f32[64,2,128,128]{3,2,1,0:T(8,128)} %bitcast.237), kind=kLoop, calls=%fused_computation.182 | loop fusion | bytes 16777216 | tf_op jit(solution)/shard_map/slice | solution.py:44
  265.2 5.6 %copy.103 = f32[64,1,128,128]{2,3,0,1:T(8,128)} copy(f32[64,1,128,128]{3,2,1,0:T(8,128)} %get-tuple-element.8) | data formatting | bytes 8388608
  270.8 5.6 %copy.102 = f32[64,1,128,128]{2,3,0,1:T(8,128)} copy(f32[64,1,128,128]{3,2,1,0:T(8,128)} %get-tuple-element.9) | data formatting | bytes 8388608
  276.4 4.2 add.206
  285.7 13.8 %all_gather.3 = f32[8,1,128,128]{3,2,1,0:T(8,128)S(1)} all-gather(f32[1,1,128,128]{3,2,1,0:T(8,128)} %copy.91), channel_id=1, replica_groups=mesh['ctx'=8,'uly'=16] {'ctx'}, dimensions={0}, use_global_device_ids=true | all-gather | bytes 589824 | tf_op jit(solution)/shard_map/all_gather | solution.py:55
  304.7 7.3 %convolution_bitcast_fusion.3 = f32[32,512,128]{1,2,0:T(8,128)} fusion(bf16[32,512,128]{2,1,0:T(8,128)(2,1)} %bitcast.27, f32[32,2,128,128]{2,3,1,0:T(8,128)} %bitcast.247), kind=kOutput, calls=%fused_computation.32 | convolution fusion | flops 536870912 | bytes 13631488 | tf_op jit(solution)/shard_map/bte,bef->btf/dot_general | solution.py:38
  312.0 8.9 %copy.72 = f32[32,512,128]{2,1,0:T(8,128)} copy(f32[32,512,128]{1,2,0:T(8,128)} %convolution_bitcast_fusion.3) | data formatting | bytes 16777216 | tf_op jit(solution)/shard_map/bte,bef->btf/dot_general | solution.py:38
  320.9 9.0 %copy.73 = f32[16384,128]{0,1:T(8,128)} copy(f32[16384,128]{1,0:T(8,128)} %bitcast.240) | data formatting | bytes 16777216 | tf_op jit(solution)/shard_map/reshape | solution.py:43
  329.9 8.0 %convolution_bitcast_fusion.4 = f32[64,256,128]{1,2,0:T(8,128)} fusion(bf16[64,256,128]{2,1,0:T(8,128)(2,1)} %bitcast.21, f32[64,1,128,128]{2,3,0,1:T(8,128)} %copy.102), kind=kOutput, calls=%fused_computation.33 | convolution fusion | flops 537919488 | bytes 16777216 | tf_op jit(solution)/shard_map/bte,bef->btf/dot_general | solution.py:38
  337.9 9.0 %copy.68 = f32[64,256,128]{2,1,0:T(8,128)} copy(f32[64,256,128]{1,2,0:T(8,128)} %convolution_bitcast_fusion.4) | data formatting | bytes 16777216 | tf_op jit(solution)/shard_map/bte,bef->btf/dot_general | solution.py:38
  346.9 9.0 %copy.69 = f32[16384,128]{0,1:T(8,128)} copy(f32[16384,128]{1,0:T(8,128)} %bitcast.241) | data formatting | bytes 16777216 | tf_op jit(solution)/shard_map/reshape | solution.py:43
  355.9 6.7 %fusion.19 = f32[16,1024,128]{1,2,0:T(8,128)} fusion(bf16[1024,16,128]{2,0,1:T(8,128)(2,1)} %all-to-all-done, f32[16,2,128,128]{2,3,1,0:T(8,128)S(1)} %bitcast.253), kind=kOutput, calls=%fused_computation.31 | convolution fusion | flops 536870912 | bytes 13107200 | tf_op jit(solution)/shard_map/bte,bef->btf/dot_general | solution.py:38
  362.6 9.2 %copy.76 = f32[16,1024,128]{2,1,0:T(8,128)} copy(f32[16,1024,128]{1,2,0:T(8,128)} %fusion.19) | data formatting | bytes 16777216 | tf_op jit(solution)/shard_map/bte,bef->btf/dot_general | solution.py:38
  371.8 9.0 %copy.77 = f32[16384,128]{0,1:T(8,128)} copy(f32[16384,128]{1,0:T(8,128)} %bitcast.242) | data formatting | bytes 16777216 | tf_op jit(solution)/shard_map/reshape | solution.py:43
  380.8 6.7 %convolution_bitcast_fusion.2 = f32[8,2048,128]{1,2,0:T(8,128)} fusion(bf16[8,2048,128]{2,1,0:T(8,128)(2,1)} %bitcast.38, f32[8,2,128,128]{2,3,1,0:T(8,128)S(1)} %bitcast.255), kind=kOutput, calls=%fused_computation.20 | convolution fusion | flops 536870912 | bytes 12845056 | tf_op jit(solution)/shard_map/bte,bef->btf/dot_general | solution.py:38
  387.5 9.1 %copy.80 = f32[8,2048,128]{2,1,0:T(8,128)} copy(f32[8,2048,128]{1,2,0:T(8,128)} %convolution_bitcast_fusion.2) | data formatting | bytes 16777216 | tf_op jit(solution)/shard_map/bte,bef->btf/dot_general | solution.py:38
  396.6 9.1 %copy.81 = f32[16384,128]{0,1:T(8,128)} copy(f32[16384,128]{1,0:T(8,128)} %bitcast.243) | data formatting | bytes 16777216 | tf_op jit(solution)/shard_map/reshape | solution.py:43
  405.7 6.7 %convolution_bitcast_fusion.1 = f32[4,4096,128]{1,2,0:T(8,128)} fusion(bf16[4,4096,128]{2,1,0:T(8,128)(2,1)} %bitcast.44, f32[4,2,128,128]{2,3,1,0:T(8,128)S(1)} %bitcast.257), kind=kOutput, calls=%fused_computation.19 | convolution fusion | flops 536870912 | bytes 12713984 | tf_op jit(solution)/shard_map/bte,bef->btf/dot_general | solution.py:38
  412.4 8.9 %copy.84 = f32[4,4096,128]{2,1,0:T(8,128)} copy(f32[4,4096,128]{1,2,0:T(8,128)} %convolution_bitcast_fusion.1) | data formatting | bytes 16777216 | tf_op jit(solution)/shard_map/bte,bef->btf/dot_general | solution.py:38
  421.2 9.0 %copy.85 = f32[16384,128]{0,1:T(8,128)} copy(f32[16384,128]{1,0:T(8,128)} %bitcast.244) | data formatting | bytes 16777216 | tf_op jit(solution)/shard_map/reshape | solution.py:43
  430.2 6.7 %convolution_bitcast_fusion = f32[2,8192,128]{1,2,0:T(8,128)} fusion(bf16[2,8192,128]{2,1,0:T(8,128)(2,1)} %bitcast.50, f32[2,2,128,128]{2,3,1,0:T(8,128)S(1)} %bitcast.260), kind=kOutput, calls=%fused_computation.13 | convolution fusion | flops 536870912 | bytes 12648448 | tf_op jit(solution)/shard_map/bte,bef->btf/dot_general | solution.py:38
  436.9 8.9 %copy.88 = f32[2,8192,128]{2,1,0:T(8,128)} copy(f32[2,8192,128]{1,2,0:T(8,128)} %convolution_bitcast_fusion) | data formatting | bytes 16777216 | tf_op jit(solution)/shard_map/bte,bef->btf/dot_general | solution.py:38
  445.8 9.1 %copy.89 = f32[16384,128]{0,1:T(8,128)} copy(f32[16384,128]{1,0:T(8,128)} %bitcast.245) | data formatting | bytes 16777216 | tf_op jit(solution)/shard_map/reshape | solution.py:43
  455.0 27.9 %fusion.7 = f32[16384,128]{0,1:T(8,128)} fusion(bf16[16384,128]{1,0:T(8,128)(2,1)} %bitcast.56, f32[16384,128]{0,1:T(8,128)} %copy.89, f32[16384,128]{0,1:T(8,128)} %copy.85, f32[16384,128]{0,1:T(8,128)} %copy.81, f32[16384,128]{0,1:T(8,128)} %copy.77, f32[16384,128]{0,1:T(8,128)} %copy.73, f32[16384,128]{0,1:T(8,128)} %copy.69, f32[16384,128]{0,1:T(8,128)} %copy.65, ...), kind=kOutput, calls=%fused_computation.11 | convolution fusion | flops 572522496 | bytes 80314368 | tf_op jit(solution)/shard_map/bte,bef->btf/dot_general | solution.py:38
  482.9 5.9 %fusion.5 = f32[16384,128]{0,1:T(8,128)S(1)} fusion(f32[16384,128]{0,1:T(8,128)} %fusion.7, bf16[16384,128]{1,0:T(8,128)(2,1)} %bitcast.56, f32[16384]{0:T(1024)S(1)} %bitcast.263, bf16[128,128]{0,1:T(8,128)(2,1)S(1)} %copy-done.17), kind=kOutput, calls=%fused_computation.8 | convolution fusion | flops 541065216 | bytes 21069824 | tf_op jit(solution)/shard_map/dot_general | solution.py:86
  488.9 3.5 fusion.3
  492.4 3.4 fusion.8
  496.3 55.5 %all_to_all.80 = bf16[16,1024,128]{1,2,0:T(8,128)(2,1)} all-to-all(bf16[16,1024,128]{1,2,0:T(8,128)(2,1)S(1)} %bitcast.248), channel_id=1, replica_groups=mesh['ctx'=8,'uly'=16] {'uly'}, dimensions={0} | all-to-all | bytes 8388608 | tf_op jit(solution)/shard_map/all_to_all | solution.py:111
  551.8 6.4 %copy.96 = bf16[1024,2048]{1,0:T(8,128)(2,1)} copy(bf16[1024,2048]{0,1:T(8,128)(2,1)} %bitcast.249) | data formatting | bytes 8388608 | tf_op jit(solution)/shard_map/all_to_all | solution.py:111
  (59 shorter events, 15.5 us)
Async XLA Ops:
  1.9 19.5 %all-to-all-start.3 = ((bf16[1024,16,12]{0,2,1:T(8,128)(2,1)}), bf16[1024,16,12]{0,2,1:T(8,128)(2,1)S(1)}, u32[]{:S(2)}, u32[]{:S(2)}) async-start(bf16[1024,16,12]{0,2,1:T(8,128)(2,1)} %all_to_all.69), calls=%async_computation.3 | async-start | bytes 1048576 | tf_op jit(solution)/shard_map/all_to_all | solution.py:104
  21.4 64.9 %all-to-all-start.1 = ((bf16[1024,16,128]{2,0,1:T(8,128)(2,1)}), bf16[1024,16,128]{2,0,1:T(8,128)(2,1)}, u32[]{:S(2)}, u32[]{:S(2)}) async-start(bf16[1024,16,128]{2,0,1:T(8,128)(2,1)} %copy_bitcast_fusion.2), calls=%async_computation.1 | async-start | bytes 8388608 | tf_op jit(solution)/shard_map/all_to_all | solution.py:102
  86.3 62.1 %all-to-all-start.2 = ((bf16[1024,16,128]{2,0,1:T(8,128)(2,1)}), bf16[1024,16,128]{2,0,1:T(8,128)(2,1)}, u32[]{:S(2)}, u32[]{:S(2)}) async-start(bf16[1024,16,128]{2,0,1:T(8,128)(2,1)} %copy_bitcast_fusion.1), calls=%async_computation.2 | async-start | bytes 8388608 | tf_op jit(solution)/shard_map/all_to_all | solution.py:103
  148.4 58.6 %all-to-all-start = ((bf16[1024,16,128]{2,0,1:T(8,128)(2,1)}), bf16[1024,16,128]{2,0,1:T(8,128)(2,1)}, u32[]{:S(2)}, u32[]{:S(2)}) async-start(bf16[1024,16,128]{2,0,1:T(8,128)(2,1)} %copy.59), calls=%async_computation | async-start | bytes 8388608 | tf_op jit(solution)/shard_map/all_to_all | solution.py:101
  280.6 2.0 copy-start
  282.7 0.8 copy-start.1
  396.6 9.1 %copy-start.2 = (f32[8,1,128,128]{2,3,0,1:T(8,128)S(1)}, f32[8,1,128,128]{2,3,0,1:T(8,128)}, u32[]{:S(2)}) copy-start(f32[8,1,128,128]{2,3,0,1:T(8,128)} %copy-done.1) | copy-start | bytes 1572868
  445.8 9.2 %copy-start.6 = (f32[1,1,16384]{2,1,0:T(1,128)S(1)}, f32[1,1,16384]{2,1,0:T(1,128)}, u32[]{:S(2)}) copy-start(f32[1,1,16384]{2,1,0:T(1,128)} %get-tuple-element.21) | copy-start | bytes 196612
  445.8 9.2 %copy-start.7 = (f32[16384]{0:T(1024)S(1)}, f32[16384]{0:T(1024)}, u32[]{:S(2)}) copy-start(f32[16384]{0:T(1024)} %get-tuple-element.28) | copy-start | bytes 196612
  445.8 9.2 %copy-start.8 = (f32[16384]{0:T(1024)S(1)}, f32[16384]{0:T(1024)}, u32[]{:S(2)}) copy-start(f32[16384]{0:T(1024)} %get-tuple-element.29) | copy-start | bytes 196612
  445.8 9.2 %copy-start.9 = (f32[16384]{0:T(1024)S(1)}, f32[16384]{0:T(1024)}, u32[]{:S(2)}) copy-start(f32[16384]{0:T(1024)} %get-tuple-element.26) | copy-start | bytes 196612
  445.8 9.2 %copy-start.10 = (f32[16384]{0:T(1024)S(1)}, f32[16384]{0:T(1024)}, u32[]{:S(2)}) copy-start(f32[16384]{0:T(1024)} %get-tuple-element.27) | copy-start | bytes 196612
  445.8 9.2 %copy-start.11 = (f32[16384]{0:T(1024)S(1)}, f32[16384]{0:T(1024)}, u32[]{:S(2)}) copy-start(f32[16384]{0:T(1024)} %get-tuple-element.24) | copy-start | bytes 196612
  445.8 9.2 %copy-start.12 = (f32[16384]{0:T(1024)S(1)}, f32[16384]{0:T(1024)}, u32[]{:S(2)}) copy-start(f32[16384]{0:T(1024)} %get-tuple-element.25) | copy-start | bytes 196612
  445.8 9.2 %copy-start.13 = (f32[16384]{0:T(1024)S(1)}, f32[16384]{0:T(1024)}, u32[]{:S(2)}) copy-start(f32[16384]{0:T(1024)} %get-tuple-element.22) | copy-start | bytes 196612
  445.8 9.2 %copy-start.14 = (f32[16384]{0:T(1024)S(1)}, f32[16384]{0:T(1024)}, u32[]{:S(2)}) copy-start(f32[16384]{0:T(1024)} %get-tuple-element.23) | copy-start | bytes 196612
  455.0 27.9 %copy-start.5 = (f32[1,1,16384]{2,1,0:T(1,128)S(1)}, f32[1,1,16384]{2,1,0:T(1,128)}, u32[]{:S(2)}) copy-start(f32[1,1,16384]{2,1,0:T(1,128)} %get-tuple-element.12) | copy-start | bytes 196612
  455.0 27.9 %copy-start.17 = (bf16[128,128]{0,1:T(8,128)(2,1)S(1)}, bf16[128,128]{0,1:T(8,128)(2,1)}, u32[]{:S(2)}) copy-start(bf16[128,128]{0,1:T(8,128)(2,1)} %copy.97) | copy-start | bytes 98308
  482.9 6.0 %copy-start.4 = (f32[1,1,16384]{2,1,0:T(1,128)S(1)}, f32[1,1,16384]{2,1,0:T(1,128)}, u32[]{:S(2)}) copy-start(f32[1,1,16384]{2,1,0:T(1,128)} %get-tuple-element.11) | copy-start | bytes 196612
  482.9 6.0 %copy-start.16 = (bf16[128,128]{0,1:T(8,128)(2,1)S(1)}, bf16[128,128]{0,1:T(8,128)(2,1)}, u32[]{:S(2)}) copy-start(bf16[128,128]{0,1:T(8,128)(2,1)} %copy.98) | copy-start | bytes 98308
  488.9 3.5 copy-start.3
  488.9 3.5 copy-start.15
where the time goes:
time: 562 us; the launch traced here: 558 us
  local copies, waits for them, and re-layouts  186 us (33%)
  waiting for transfers between devices  144 us (26%)
  matrix products  115 us (20%)
  blocking collectives  69.3 us (12%)
  other arithmetic  22 us (4%)
  starting transfers between devices  21.8 us (4%)
    dot_general x8, matrix products, head_levels(): jnp.einsum('bte,bef->btf', pair_queries, earlier, preferred_element_type=...  79 us
    reshape x7, local copies, waits for them, and re-layouts, head_levels(): partial_value.reshape(row_total, HEAD_DIM) * factor[:, None]  63.1 us
    all_to_all x1, blocking collectives, shards(): lax.all_to_all(result, 'uly', split_axis=0, concat_axis=1, tiled=True)  55.5 us
    all_to_all x1, waiting for transfers between devices, shards(): lax.all_to_all(key_vectors, 'uly', split_axis=1, concat_axis=0, tiled=True)  55.1 us
    dot_general x6, local copies, waits for them, and re-layouts, head_levels(): jnp.einsum('bte,bef->btf', pair_queries, earlier, preferred_element_type=...  54.1 us
    all_to_all x1, waiting for transfers between devices, shards(): lax.all_to_all(value_vectors, 'uly', split_axis=1, concat_axis=0, tiled=T...  44 us
    all_to_all x1, waiting for transfers between devices, shards(): lax.all_to_all(queries, 'uly', split_axis=1, concat_axis=0, tiled=True)  38.2 us
    unnamed x42, local copies, waits for them, and re-layouts  24.4 us
  transfers between devices with their start and end apart: 4, of which 4 were waited for; matrix products, arithmetic and copies ran while one was open for 7% of the time, Pallas kernels for 0%

commit v1 on v0

v1 whole, which is shorter than its diff:
```python
import functools
import jax
import jax.numpy as jnp
from jax import lax
from jax.experimental import pallas as pl
from jax.experimental.pallas import tpu as pltpu
from jax.sharding import PartitionSpec as P

D = 128
BLOCK = 64
TILE = 256
LEVELS = 12
FIRST_REMOTE = 5
STEPS = 7
HC = 2
LAG = 3
F32 = jnp.float32
BF16 = jnp.bfloat16
MESH = pl.DeviceIdType.MESH


def dot_nt(a, b):
    return lax.dot_general(a, b, (((1,), (1,)), ((), ())), preferred_element_type=F32)


def dot_nn(a, b):
    return lax.dot_general(a, b, (((1,), (0,)), ((), ())), preferred_element_type=F32)


def kernel(
    heads,
    q_hbm, k_hbm, v_hbm, g_hbm, o_hbm,
    q_s, k_s, v_s, g_s, vt_s, gate_s, acc_s, cur_s, near_s, send_s, recv_s, out_s,
    in_sem, gate_sem, out_sem, send_sem, recv_sem,
):
    rows = q_s.shape[0]
    tiles = rows // TILE
    chunks = heads // HC
    wide = HC * D

    ctx = lax.axis_index("ctx")
    uly = lax.axis_index("uly")
    core, y = ctx % 2, ctx // 2
    x, z = uly % 4, uly // 4
    x_flip = x + 1 - 2 * (x % 2)
    z_flip = z + 1 - 2 * (z % 2)
    y_flip = y + 1 - 2 * (y % 2)
    partners = (
        (ctx, z * 4 + x_flip),
        (ctx, z * 4 + 3 - x),
        (ctx, z_flip * 4 + x),
        (ctx, (3 - z) * 4 + x),
        (y * 2 + 1 - core, uly),
        (y_flip * 2 + core, uly),
        ((3 - y) * 2 + core, uly),
    )
    bits = (x % 2, x // 2, z % 2, z // 2, core, y % 2, y // 2)

    def columns(c):
        return pl.ds(pl.multiple_of(c * wide, wide), wide)

    def load(which, c):
        hbm, vmem = ((k_hbm, k_s), (v_hbm, v_s), (q_hbm, q_s))[which]
        return pltpu.make_async_copy(
            hbm.at[:, columns(c)], vmem.at[:, columns(c)], in_sem.at[which, c]
        )

    def store(h):
        cols = pl.ds(pl.multiple_of(h * D, D), D)
        return pltpu.make_async_copy(out_s.at[:, cols], o_hbm.at[:, cols], out_sem.at[h])

    def message(step, c):
        part = pl.ds(c * HC, HC)
        return pltpu.make_async_remote_copy(
            src_ref=send_s.at[step, part],
            dst_ref=recv_s.at[step, part],
            send_sem=send_sem.at[step, c],
            recv_sem=recv_sem.at[step, c],
            device_id=partners[step],
            device_id_type=MESH,
        )

    gate_load = pltpu.make_async_copy(g_hbm, g_s, gate_sem)
    gate_load.start()

    @pl.loop(0, chunks)
    def _(c):
        load(0, c).start()
        load(1, c).start()

    @pl.loop(0, chunks)
    def _(c):
        load(2, c).start()

    barrier = pltpu.get_barrier_semaphore()
    for partner in partners:
        pl.semaphore_signal(barrier, inc=1, device_id=partner, device_id_type=MESH)

    gate_load.wait()
    row = lax.broadcasted_iota(jnp.int32, (heads * 16, heads * LEVELS), 0)
    col = lax.broadcasted_iota(jnp.int32, (heads * 16, heads * LEVELS), 1)
    pick = (col == (row // 16) * LEVELS + row % 16) & (row % 16 < LEVELS)
    table = dot_nt(jnp.where(pick, 1.0, 0.0).astype(BF16), g_s[...])
    level = lax.broadcasted_iota(jnp.int32, (heads * 16, 1), 0) % 16
    scale = jnp.zeros((heads * 16, 1), F32)
    for l in range(LEVELS):
        factor = jnp.float32((BLOCK * 2 ** max(l - 1, 0)) ** -0.5)
        if l >= FIRST_REMOTE:
            factor = factor * bits[l - FIRST_REMOTE].astype(F32)
        scale = jnp.where(level == l, factor, scale)
    gate_s[...] = (table * scale).reshape(heads, 16, rows)

    pl.semaphore_wait(barrier, STEPS)

    def states(c):
        load(0, c).wait()
        load(1, c).wait()
        for part in range(HC):
            h = c * HC + part
            cols = pl.ds(pl.multiple_of(h * D, D), D)
            vt = v_s[:, cols].T
            vt_s[h] = vt
            sums = [
                dot_nn(vt[:, i * TILE:(i + 1) * TILE], k_s[i * TILE:(i + 1) * TILE, cols])
                for i in range(tiles)
            ]
            first = sums[0] + sums[1]
            near_s[h, 0] = sums[0].astype(BF16)
            near_s[h, 1] = sums[2].astype(BF16)
            near_s[h, 2] = first.astype(BF16)
            total = first + (sums[2] + sums[3])
            cur_s[h] = total
            send_s[0, h] = total.astype(BF16)
        message(0, c).start()

    def exchange(step, c):
        message(step, c).wait_recv()
        if step + 1 < STEPS:
            for part in range(HC):
                h = c * HC + part
                total = cur_s[h] + recv_s[step, h].astype(F32)
                cur_s[h] = total
                send_s[step + 1, h] = total.astype(BF16)
            message(step + 1, c).start()

    def exchanges(slot):
        for step in reversed(range(STEPS)):
            c = slot - LAG * (step + 1)

            @pl.when((c >= 0) & (c < chunks))
            def _():
                exchange(step, c)

    half = TILE // 2
    s_at = lax.broadcasted_iota(jnp.int32, (half, half), 0)
    t_at = lax.broadcasted_iota(jnp.int32, (half, half), 1)
    own = (s_at // BLOCK == t_at // BLOCK) & (s_at <= t_at)
    before = s_at // BLOCK < t_at // BLOCK

    def local(h):
        cols = pl.ds(pl.multiple_of(h * D, D), D)
        for i in range(tiles):
            span = slice(i * TILE, (i + 1) * TILE)
            q_tile = q_s[span, cols]
            scores = dot_nt(k_s[span, cols], q_tile)
            gate = [gate_s[h, l:l + 1, span] for l in range(FIRST_REMOTE)]

            def weigh(at):
                part = slice(at, at + half)
                return jnp.where(own, gate[0][:, part], jnp.where(before, gate[1][:, part], 0.0))

            top = jnp.concatenate(
                [scores[:half, :half] * weigh(0), scores[:half, half:] * gate[2][:, half:]], axis=1
            )
            low = jnp.concatenate(
                [jnp.zeros((half, half), F32), scores[half:, half:] * weigh(half)], axis=1
            )
            weights = jnp.concatenate([top.astype(BF16), low.astype(BF16)], axis=0)
            out = dot_nn(vt_s[h, :, span], weights)
            if i % 2 == 1:
                out = out + dot_nt(near_s[h, i // 2], q_tile) * gate[3]
            if i >= 2:
                out = out + dot_nt(near_s[h, 2], q_tile) * gate[4]
            acc_s[h, :, span] = out

    def remote(h):
        cols = pl.ds(pl.multiple_of(h * D, D), D)
        for i in range(tiles):
            span = slice(i * TILE, (i + 1) * TILE)
            q_tile = q_s[span, cols]
            out = acc_s[h, :, span]
            for step in range(STEPS):
                l = FIRST_REMOTE + step
                out = out + dot_nt(recv_s[step, h], q_tile) * gate_s[h, l:l + 1, span]
            out_s[span, cols] = out.T.astype(BF16)
        store(h).start()

    @pl.loop(0, chunks)
    def _(c):
        states(c)
        exchanges(c)

    @pl.loop(0, chunks)
    def _(c):
        load(2, c).wait()

    @pl.loop(0, heads)
    def _(h):
        local(h)
        exchanges(chunks + h)

    @pl.loop(0, heads)
    def _(h):
        exchanges(chunks + heads + h)
        remote(h)

    @pl.loop(0, heads)
    def _(h):
        store(h).wait()

    for step in range(STEPS):
        @pl.loop(0, chunks)
        def _(c):
            message(step, c).wait_send()


def shards(queries, key_vectors, value_vectors, level_gates):
    rows, width = queries.shape
    heads = width // D
    chunks = heads // HC
    hbm = pl.BlockSpec(memory_space=pl.ANY)
    return pl.pallas_call(
        functools.partial(kernel, heads),
        out_shape=jax.ShapeDtypeStruct((rows, width), BF16),
        in_specs=[hbm] * 4,
        out_specs=hbm,
        scratch_shapes=[
            pltpu.VMEM((rows, width), BF16),
            pltpu.VMEM((rows, width), BF16),
            pltpu.VMEM((rows, width), BF16),
            pltpu.VMEM((rows, heads * LEVELS), BF16),
            pltpu.VMEM((heads, D, rows), BF16),
            pltpu.VMEM((heads, 16, rows), F32),
            pltpu.VMEM((heads, D, rows), F32),
            pltpu.VMEM((heads, D, D), F32),
            pltpu.VMEM((heads, 3, D, D), BF16),
            pltpu.VMEM((STEPS, heads, D, D), BF16),
            pltpu.VMEM((STEPS, heads, D, D), BF16),
            pltpu.VMEM((rows, width), BF16),
            pltpu.SemaphoreType.DMA((3, chunks)),
            pltpu.SemaphoreType.DMA,
            pltpu.SemaphoreType.DMA((heads,)),
            pltpu.SemaphoreType.DMA((STEPS, chunks)),
            pltpu.SemaphoreType.DMA((STEPS, chunks)),
        ],
        compiler_params=pltpu.CompilerParams(
            collective_id=0, has_side_effects=True, vmem_limit_bytes=56 * 1024 * 1024
        ),
        name="fenwick",
    )(queries, key_vectors, value_vectors, level_gates)


def solution(mesh):
    spec = P(("ctx", "uly"), None)
    return jax.shard_map(
        shards, mesh=mesh, in_specs=(spec,) * 4, out_specs=spec, check_vma=False
    )
```

time: 562 us -> 63.5 us (0.11)
  local copies, waits for them, and re-layouts: 186 us -> 6.78 us
  waiting for transfers between devices: 144 us -> 0 us
  matrix products: 115 us -> 0 us
  blocking collectives: 69.3 us -> 0 us
  Pallas kernels: 0 us -> 56.6 us
  other arithmetic: 22 us -> 0 us
  starting transfers between devices: 21.8 us -> 0 us
    all_to_all x4 -> x0, waiting for transfers between devices: 144 us -> none  [the longest x1 55.1 us: shards(): lax.all_to_all(key_vectors, 'uly', split_axis=1, concat_axis=0, tiled=True)]
    dot_general x13 -> x0, matrix products: 115 us -> none  [the longest x8 79 us: head_levels(): jnp.einsum('bte,bef->btf', pair_queries, earlier, preferred_element_type=...]
    reshape x8 -> x0, local copies, waits for them, and re-layouts: 72 us -> none  [the longest x7 63.1 us: head_levels(): partial_value.reshape(row_total, HEAD_DIM) * factor[:, None]]
    pallas_call x0 -> x1, Pallas kernels: none -> 56.6 us  [shards(): pl.pallas_call(functools.partial(kernel, heads), out_shape=jax.ShapeDtype...]
    all_to_all x1 -> x0, blocking collectives: 55.5 us -> none  [shards(): lax.all_to_all(result, 'uly', split_axis=0, concat_axis=1, tiled=True)]
    dot_general x6 -> x0, local copies, waits for them, and re-layouts: 54.1 us -> none  [head_levels(): jnp.einsum('bte,bef->btf', pair_queries, earlier, preferred_element_type=...]
    all_to_all x6 -> x0, local copies, waits for them, and re-layouts: 25.5 us -> none  [the longest x2 6.86 us: shards(): lax.all_to_all(result, 'uly', split_axis=0, concat_axis=1, tiled=True)]
    all_to_all x4 -> x0, starting transfers between devices: 21.8 us -> none  [the longest x1 7.96 us: shards(): lax.all_to_all(level_gates, 'uly', split_axis=1, concat_axis=0, tiled=True)]
  transfers between devices with their start and end apart: 4 -> 0, of which waited for: 4 -> 0; matrix products, arithmetic and copies ran while one was open for 7% -> 0% of each run, Pallas kernels for 0% -> 0%
where the time goes in v1:
time: 63.5 us; the launch traced here: 63.4 us
  Pallas kernels  56.6 us (89%)
  local copies, waits for them, and re-layouts  6.78 us (11%)
    pallas_call x1, Pallas kernels, shards(): pl.pallas_call(functools.partial(kernel, heads), out_shape=jax.ShapeDtype...  56.6 us
    unnamed x2, local copies, waits for them, and re-layouts  6.78 us

profile of v1, /device:TPU:0, one launch (start us, length us, event | category | flops | bytes accessed | tf_op | source)
XLA Modules:
  0.0 63.4 jit_solution(11166682526997946015)
XLA Ops:
  0.0 2.0 %copy.5.g_hbm = bf16[1024,192]{1,0:T(8,128)(2,1)} copy(bf16[1024,192]{0,1:T(8,128)(2,1)} %param.7) | data formatting | bytes 786432 | tf_op args[3]
  2.0 56.6 %fenwick.1 = bf16[1024,2048]{1,0:T(8,128)(2,1)} custom-call(bf16[1024,2048]{1,0:T(8,128)(2,1)} %q_hbm.1, bf16[1024,2048]{1,0:T(8,128)(2,1)} %k_hbm.1, bf16[1024,2048]{1,0:T(8,128)(2,1)} %v_hbm.1, bf16[1024,192]{1,0:T(8,128)(2,1)} %copy.5.g_hbm), custom_call_target="tpu_custom_call" | custom-call | tf_op jit(solution)/shard_map/fenwick/pallas_call | solution.py:232
  58.6 4.8 %copy.7 = bf16[1024,2048]{1,0:T(8,128)(2,1)} copy(bf16[1024,2048]{1,0:T(8,128)(2,1)} %fenwick.1) | data formatting | bytes 8388608

commit v2 on v1

v2 whole, which is shorter than its diff:
```python
import functools
import jax
import jax.numpy as jnp
from jax import lax
from jax.experimental import pallas as pl
from jax.experimental.pallas import tpu as pltpu
from jax.sharding import PartitionSpec as P

D = 128
BLOCK = 64
TILE = 256
LEVELS = 12
FIRST_REMOTE = 5
STEPS = 7
HC = 2
VL = 58
OFF = (3, 6, 9, 12, 15, 18, 21)
LP = 2
F32 = jnp.float32
BF16 = jnp.bfloat16
MESH = pl.DeviceIdType.MESH


def dot_nt(a, b):
    return lax.dot_general(a, b, (((1,), (1,)), ((), ())), preferred_element_type=F32)


def dot_nn(a, b):
    return lax.dot_general(a, b, (((1,), (0,)), ((), ())), preferred_element_type=F32)


def kernel(
    heads,
    q_hbm, k_hbm, v_hbm, g_hbm, o_ref,
    q_s, k_s, v_s, g_s, gate_s, acc_s, cur_s, near_s, send_s, recv_s,
    in_sem, gate_sem, send_sem, recv_sem,
):
    rows = q_s.shape[0]
    tiles = rows // TILE
    chunks = heads // HC
    wide = HC * D

    ctx = lax.axis_index("ctx")
    uly = lax.axis_index("uly")
    core, y = ctx % 2, ctx // 2
    x, z = uly % 4, uly // 4
    x_flip = x + 1 - 2 * (x % 2)
    z_flip = z + 1 - 2 * (z % 2)
    y_flip = y + 1 - 2 * (y % 2)
    partners = (
        (ctx, z * 4 + x_flip),
        (ctx, z * 4 + 3 - x),
        (ctx, z_flip * 4 + x),
        (ctx, (3 - z) * 4 + x),
        (y * 2 + 1 - core, uly),
        (y_flip * 2 + core, uly),
        ((3 - y) * 2 + core, uly),
    )
    bits = (x % 2, x // 2, z % 2, z // 2, core, y % 2, y // 2)

    def columns(c):
        return pl.ds(pl.multiple_of(c * wide, wide), wide)

    def load(which, c):
        hbm, vmem = ((k_hbm, k_s), (v_hbm, v_s), (q_hbm, q_s))[which]
        return pltpu.make_async_copy(
            hbm.at[:, columns(c)], vmem.at[:, columns(c)], in_sem.at[which, c]
        )

    def message(step, c):
        return pltpu.make_async_remote_copy(
            src_ref=send_s.at[step, c],
            dst_ref=recv_s.at[step, c],
            send_sem=send_sem.at[step, c],
            recv_sem=recv_sem.at[step, c],
            device_id=partners[step],
            device_id_type=MESH,
        )

    gate_load = pltpu.make_async_copy(g_hbm, g_s, gate_sem)
    gate_load.start()

    @pl.loop(0, chunks)
    def _(c):
        load(0, c).start()
        load(1, c).start()

    @pl.loop(0, chunks)
    def _(c):
        load(2, c).start()

    barrier = pltpu.get_barrier_semaphore()
    for partner in partners:
        pl.semaphore_signal(barrier, inc=1, device_id=partner, device_id_type=MESH)

    pl.semaphore_wait(barrier, STEPS)

    def states(c):
        load(0, c).wait()
        load(1, c).wait()
        for part in range(HC):
            h = c * HC + part
            cols = pl.ds(pl.multiple_of(h * D, D), D)
            vt = v_s[:, cols].T
            sums = [
                dot_nn(vt[:, i * TILE:(i + 1) * TILE], k_s[i * TILE:(i + 1) * TILE, cols])
                for i in range(tiles)
            ]
            first = sums[0] + sums[1]
            near_s[h, 0] = sums[0].astype(BF16)
            near_s[h, 1] = sums[2].astype(BF16)
            near_s[h, 2] = first.astype(BF16)
            total = first + (sums[2] + sums[3])
            cur_s[h] = total
            send_s[0, c, part * D:(part + 1) * D] = total.astype(BF16)
        message(0, c).start()

    def exchange(step, c):
        message(step, c).wait_recv()
        if step + 1 < STEPS:
            for part in range(HC):
                h = c * HC + part
                total = cur_s[h] + recv_s[step, c, part * D:(part + 1) * D].astype(F32)
                cur_s[h] = total
                send_s[step + 1, c, part * D:(part + 1) * D] = total.astype(BF16)
            message(step + 1, c).start()

    def exchanges(slot):
        for step in reversed(range(STEPS)):
            c = slot - OFF[step]

            @pl.when((c >= 0) & (c < chunks))
            def _():
                exchange(step, c)

    half = TILE // 2
    s_at = lax.broadcasted_iota(jnp.int32, (half, half), 0)
    t_at = lax.broadcasted_iota(jnp.int32, (half, half), 1)
    own = (s_at // BLOCK == t_at // BLOCK) & (s_at <= t_at)
    before = s_at // BLOCK < t_at // BLOCK

    def local(h):
        cols = pl.ds(pl.multiple_of(h * D, D), D)
        for i in range(tiles):
            span = slice(i * TILE, (i + 1) * TILE)
            q_tile = q_s[span, cols]
            scores = dot_nt(k_s[span, cols], q_tile)
            gate = [gate_s[h, l:l + 1, span] for l in range(3)]

            def weigh(at):
                part = slice(at, at + half)
                return jnp.where(own, gate[0][:, part], jnp.where(before, gate[1][:, part], 0.0))

            top = jnp.concatenate(
                [scores[:half, :half] * weigh(0), scores[:half, half:] * gate[2][:, half:]], axis=1
            )
            low = jnp.concatenate(
                [jnp.zeros((half, half), F32), scores[half:, half:] * weigh(half)], axis=1
            )
            weights = jnp.concatenate([top.astype(BF16), low.astype(BF16)], axis=0)
            acc_s[h, span] = dot_nn(weights.T, v_s[span, cols])

    def remote(c, part):
        h = c * HC + part
        cols = pl.ds(pl.multiple_of(h * D, D), D)
        for i in range(tiles):
            span = slice(i * TILE, (i + 1) * TILE)
            q_tile = q_s[span, cols]
            parts = [(FIRST_REMOTE + st, recv_s[st, c, part * D:(part + 1) * D]) for st in range(STEPS)]
            if i % 2 == 1:
                parts.append((3, near_s[h, i // 2]))
            if i >= 2:
                parts.append((4, near_s[h, 2]))
            reads = dot_nt(jnp.concatenate([state for _, state in parts], axis=0), q_tile)
            total = jnp.zeros((D, TILE), F32)
            for at, (l, _) in enumerate(parts):
                total = total + reads[at * D:(at + 1) * D] * gate_s[h, l:l + 1, span]
            o_ref[span, cols] = (total.T + acc_s[h, span]).astype(BF16)

    @pl.loop(0, chunks)
    def _(c):
        exchanges(c)
        states(c)

    gate_load.wait()
    row = lax.broadcasted_iota(jnp.int32, (heads * 16, heads * LEVELS), 0)
    col = lax.broadcasted_iota(jnp.int32, (heads * 16, heads * LEVELS), 1)
    pick = (col == (row // 16) * LEVELS + row % 16) & (row % 16 < LEVELS)
    table = dot_nn(jnp.where(pick, 1.0, 0.0).astype(BF16), g_s[...])
    level = lax.broadcasted_iota(jnp.int32, (heads * 16, 1), 0) % 16
    scale = jnp.zeros((heads * 16, 1), F32)
    for l in range(LEVELS):
        factor = jnp.float32((BLOCK * 2 ** max(l - 1, 0)) ** -0.5)
        if l >= FIRST_REMOTE:
            factor = factor * bits[l - FIRST_REMOTE].astype(F32)
        scale = jnp.where(level == l, factor, scale)
    gate_s[...] = (table * scale).reshape(heads, 16, rows)

    @pl.loop(0, chunks)
    def _(c):
        load(2, c).wait()

    @pl.loop(0, heads // LP)
    def _(n):
        exchanges(chunks + n)
        for part in range(LP):
            local(n * LP + part)

    done = chunks + heads // LP
    idle = max(0, OFF[-1] - done)

    @pl.loop(0, idle)
    def _(n):
        exchanges(done + n)

    @pl.loop(0, chunks)
    def _(c):
        exchanges(done + idle + c)
        for part in range(HC):
            remote(c, part)

    for step in range(STEPS):
        @pl.loop(0, chunks)
        def _(c):
            message(step, c).wait_send()


def shards(queries, key_vectors, value_vectors, level_gates):
    rows, width = queries.shape
    heads = width // D
    chunks = heads // HC
    hbm = pl.BlockSpec(memory_space=pltpu.HBM)
    return pl.pallas_call(
        functools.partial(kernel, heads),
        out_shape=pltpu.VMEM((rows, width), BF16),
        in_specs=[hbm] * 4,
        out_specs=pl.BlockSpec(memory_space=pltpu.VMEM),
        scratch_shapes=[
            pltpu.VMEM((rows, width), BF16),
            pltpu.VMEM((rows, width), BF16),
            pltpu.VMEM((rows, width), BF16),
            pltpu.VMEM((heads * LEVELS, rows), BF16),
                        pltpu.VMEM((heads, 16, rows), F32),
            pltpu.VMEM((heads, rows, D), F32),
            pltpu.VMEM((heads, D, D), F32),
            pltpu.VMEM((heads, 3, D, D), BF16),
            pltpu.VMEM((STEPS, chunks, HC * D, D), BF16),
            pltpu.VMEM((STEPS, chunks, HC * D, D), BF16),
            pltpu.SemaphoreType.DMA((3, chunks)),
            pltpu.SemaphoreType.DMA,
            pltpu.SemaphoreType.DMA((STEPS, chunks)),
            pltpu.SemaphoreType.DMA((STEPS, chunks)),
        ],
        compiler_params=pltpu.CompilerParams(
            collective_id=0, has_side_effects=True, vmem_limit_bytes=VL * 1024 * 1024
        ),
        name="fenwick",
    )(queries, key_vectors, value_vectors, level_gates.T)


def solution(mesh):
    spec = P(("ctx", "uly"), None)
    return jax.shard_map(
        shards, mesh=mesh, in_specs=(spec,) * 4, out_specs=spec, check_vma=False
    )
```

time: 63.5 us -> 51.1 us (0.80)
  Pallas kernels: 56.6 us -> 49 us
  local copies, waits for them, and re-layouts: 6.78 us -> 2.02 us
    pallas_call x1, Pallas kernels: 56.6 us -> 49 us  [shards(): pl.pallas_call(functools.partial(kernel, heads), out_shape=pltpu.VMEM((ro...]
    unnamed x2 -> x1, local copies, waits for them, and re-layouts: 6.78 us -> 2.02 us
where the time goes in v2:
time: 51.1 us; the launch traced here: 51 us
  Pallas kernels  49 us (96%)
  local copies, waits for them, and re-layouts  2.02 us (4%)
    pallas_call x1, Pallas kernels, shards(): pl.pallas_call(functools.partial(kernel, heads), out_shape=pltpu.VMEM((ro...  49 us
    unnamed x1, local copies, waits for them, and re-layouts  2.02 us

profile of v2, /device:TPU:0, one launch (start us, length us, event | category | flops | bytes accessed | tf_op | source)
XLA Modules:
  0.0 51.0 jit_solution(16720528215714976399)
XLA Ops:
  0.0 49.0 %fenwick.1 = bf16[1024,2048]{1,0:T(8,128)(2,1)S(1)} custom-call(bf16[1024,2048]{1,0:T(8,128)(2,1)} %q_hbm.1, bf16[1024,2048]{1,0:T(8,128)(2,1)} %k_hbm.1, bf16[1024,2048]{1,0:T(8,128)(2,1)} %v_hbm.1, bf16[192,1024]{1,0:T(8,128)(2,1)} %bitcast.1), custom_call_target="tpu_custom_call" | custom-call | tf_op jit(solution)/shard_map/fenwick/pallas_call | solution.py:233
  49.0 2.0 %copy.6 = bf16[1024,2048]{1,0:T(8,128)(2,1)} copy(bf16[1024,2048]{1,0:T(8,128)(2,1)S(1)} %fenwick.1) | data formatting | bytes 8388608

commit v3 on v2

--- a/solution.py
+++ b/solution.py
@@ -12,9 +12,11 @@
 LEVELS = 12
 FIRST_REMOTE = 5
 STEPS = 7
+UNIFORM = 5
 HC = 2
+GS = 2
 VL = 58
-OFF = (3, 6, 9, 12, 15, 18, 21)
+OFF = (4, 7, 10, 13, 14, 16, 17)
 LP = 2
 F32 = jnp.float32
 BF16 = jnp.bfloat16
@@ -32,7 +34,7 @@
 def kernel(
     heads,
     q_hbm, k_hbm, v_hbm, g_hbm, o_ref,
-    q_s, k_s, v_s, g_s, gate_s, acc_s, cur_s, near_s, send_s, recv_s,
+    q_s, k_s, v_s, g_s, gate_s, acc_s, cur_s, near_s, send_s, recv_s, pair_s, side_s,
     in_sem, gate_sem, send_sem, recv_sem,
 ):
     rows = q_s.shape[0]
@@ -47,6 +49,7 @@
     x_flip = x + 1 - 2 * (x % 2)
     z_flip = z + 1 - 2 * (z % 2)
     y_flip = y + 1 - 2 * (y % 2)
+    y_far = y + 2 - 4 * (y // 2)
     partners = (
         (ctx, z * 4 + x_flip),
         (ctx, z * 4 + 3 - x),
@@ -55,8 +58,11 @@
         (y * 2 + 1 - core, uly),
         (y_flip * 2 + core, uly),
         ((3 - y) * 2 + core, uly),
+        (y_far * 2 + core, uly),
     )
     bits = (x % 2, x // 2, z % 2, z // 2, core, y % 2, y // 2)
+
+    sends = (y % 2 == 0, y < 2, y < 2)
 
     def columns(c):
         return pl.ds(pl.multiple_of(c * wide, wide), wide)
@@ -77,6 +83,27 @@
             device_id_type=MESH,
         )
 
+    def column(k, c):
+        span = pl.ds(0, HC * D)
+        return pltpu.make_async_remote_copy(
+            src_ref=send_s.at[UNIFORM, c],
+            dst_ref=pair_s.at[c, span] if k == 0 else side_s.at[k - 1, c],
+            send_sem=send_sem.at[UNIFORM + k, c],
+            recv_sem=recv_sem.at[UNIFORM + k, c],
+            device_id=partners[UNIFORM + k],
+            device_id_type=MESH,
+        )
+
+    def forward(c):
+        return pltpu.make_async_remote_copy(
+            src_ref=pair_s.at[c],
+            dst_ref=pair_s.at[c],
+            send_sem=send_sem.at[UNIFORM + 3, c],
+            recv_sem=recv_sem.at[UNIFORM + 3, c],
+            device_id=partners[UNIFORM - 1],
+            device_id_type=MESH,
+        )
+
     gate_load = pltpu.make_async_copy(g_hbm, g_s, gate_sem)
     gate_load.start()
 
@@ -89,11 +116,12 @@
     def _(c):
         load(2, c).start()
 
+    pair_s[...] = jnp.zeros_like(pair_s)
     barrier = pltpu.get_barrier_semaphore()
     for partner in partners:
         pl.semaphore_signal(barrier, inc=1, device_id=partner, device_id_type=MESH)
 
-    pl.semaphore_wait(barrier, STEPS)
+    pl.semaphore_wait(barrier, len(partners))
 
     def states(c):
         load(0, c).wait()
@@ -115,15 +143,50 @@
             send_s[0, c, part * D:(part + 1) * D] = total.astype(BF16)
         message(0, c).start()
 
+    def advance(step, c):
+        for part in range(HC):
+            h = c * HC + part
+            rows_of = slice(part * D, (part + 1) * D)
+            total = cur_s[h] + recv_s[step, c, rows_of].astype(F32)
+            cur_s[h] = total
+            send_s[step + 1, c, rows_of] = total.astype(BF16)
+
     def exchange(step, c):
-        message(step, c).wait_recv()
-        if step + 1 < STEPS:
-            for part in range(HC):
-                h = c * HC + part
-                total = cur_s[h] + recv_s[step, c, part * D:(part + 1) * D].astype(F32)
-                cur_s[h] = total
-                send_s[step + 1, c, part * D:(part + 1) * D] = total.astype(BF16)
+        owner = core == c % 2
+        if step < UNIFORM:
+            message(step, c).wait_recv()
+        if step + 1 < UNIFORM:
+            advance(step, c)
             message(step + 1, c).start()
+        elif step + 1 == UNIFORM:
+
+            @pl.when(owner)
+            def _():
+                advance(step, c)
+                for k in range(3):
+                    pl.when(sends[k])(column(k, c).start)
+
+        elif step == UNIFORM:
+
+            @pl.when(owner)
+            def _():
+                pl.when(y % 2 == 1)(column(0, c).wait_recv)
+
+                @pl.when(y >= 2)
+                def _():
+                    column(1, c).wait_recv()
+                    column(2, c).wait_recv()
+                    pair_s[c, HC * D:] = (
+                        side_s[0, c].astype(F32) + side_s[1, c].astype(F32)
+                    ).astype(BF16)
+
+                forward(c).start()
+
+        else:
+
+            @pl.when(core != c % 2)
+            def _():
+                forward(c).wait_recv()
 
     def exchanges(slot):
         for step in reversed(range(STEPS)):
@@ -132,6 +195,21 @@
             @pl.when((c >= 0) & (c < chunks))
             def _():
                 exchange(step, c)
+
+    def gates():
+        gate_load.wait()
+        row = lax.broadcasted_iota(jnp.int32, (heads * 16, heads * LEVELS), 0)
+        col = lax.broadcasted_iota(jnp.int32, (heads * 16, heads * LEVELS), 1)
+        pick = (col == (row // 16) * LEVELS + row % 16) & (row % 16 < LEVELS)
+        table = dot_nn(jnp.where(pick, 1.0, 0.0).astype(BF16), g_s[...])
+        level = lax.broadcasted_iota(jnp.int32, (heads * 16, 1), 0) % 16
+        scale = jnp.zeros((heads * 16, 1), F32)
+        for l in range(LEVELS):
+            factor = jnp.float32((BLOCK * 2 ** max(l - 1, 0)) ** -0.5)
+            if l >= FIRST_REMOTE:
+                factor = factor * bits[l - FIRST_REMOTE].astype(F32)
+            scale = jnp.where(level == l, factor, scale)
+        gate_s[...] = (table * scale).reshape(heads, 16, rows)
 
     half = TILE // 2
     s_at = lax.broadcasted_iota(jnp.int32, (half, half), 0)
@@ -166,7 +244,10 @@
         for i in range(tiles):
             span = slice(i * TILE, (i + 1) * TILE)
             q_tile = q_s[span, cols]
-            parts = [(FIRST_REMOTE + st, recv_s[st, c, part * D:(part + 1) * D]) for st in range(STEPS)]
+            parts = [(FIRST_REMOTE + st, recv_s[st, c, part * D:(part + 1) * D]) for st in range(UNIFORM)]
+            for st in range(UNIFORM, STEPS):
+                at = (st - UNIFORM) * HC * D + part * D
+                parts.append((FIRST_REMOTE + st, pair_s[c, at:at + D]))
             if i % 2 == 1:
                 parts.append((3, near_s[h, i // 2]))
             if i >= 2:
@@ -182,19 +263,9 @@
         exchanges(c)
         states(c)
 
-    gate_load.wait()
-    row = lax.broadcasted_iota(jnp.int32, (heads * 16, heads * LEVELS), 0)
-    col = lax.broadcasted_iota(jnp.int32, (heads * 16, heads * LEVELS), 1)
-    pick = (col == (row // 16) * LEVELS + row % 16) & (row % 16 < LEVELS)
-    table = dot_nn(jnp.where(pick, 1.0, 0.0).astype(BF16), g_s[...])
-    level = lax.broadcasted_iota(jnp.int32, (heads * 16, 1), 0) % 16
-    scale = jnp.zeros((heads * 16, 1), F32)
-    for l in range(LEVELS):
-        factor = jnp.float32((BLOCK * 2 ** max(l - 1, 0)) ** -0.5)
-        if l >= FIRST_REMOTE:
-            factor = factor * bits[l - FIRST_REMOTE].astype(F32)
-        scale = jnp.where(level == l, factor, scale)
-    gate_s[...] = (table * scale).reshape(heads, 16, rows)
+        @pl.when(c == GS)
+        def _():
+            gates()
 
     @pl.loop(0, chunks)
     def _(c):
@@ -219,10 +290,16 @@
         for part in range(HC):
             remote(c, part)
 
-    for step in range(STEPS):
-        @pl.loop(0, chunks)
-        def _(c):
+    @pl.loop(0, chunks)
+    def _(c):
+        for step in range(UNIFORM):
             message(step, c).wait_send()
+
+        @pl.when(core == c % 2)
+        def _():
+            for k in range(3):
+                pl.when(sends[k])(column(k, c).wait_send)
+            forward(c).wait_send()
 
 
 def shards(queries, key_vectors, value_vectors, level_gates):
@@ -240,16 +317,18 @@
             pltpu.VMEM((rows, width), BF16),
             pltpu.VMEM((rows, width), BF16),
             pltpu.VMEM((heads * LEVELS, rows), BF16),
-                        pltpu.VMEM((heads, 16, rows), F32),
+            pltpu.VMEM((heads, 16, rows), F32),
             pltpu.VMEM((heads, rows, D), F32),
             pltpu.VMEM((heads, D, D), F32),
             pltpu.VMEM((heads, 3, D, D), BF16),
-            pltpu.VMEM((STEPS, chunks, HC * D, D), BF16),
-            pltpu.VMEM((STEPS, chunks, HC * D, D), BF16),
+            pltpu.VMEM((UNIFORM + 1, chunks, HC * D, D), BF16),
+            pltpu.VMEM((UNIFORM, chunks, HC * D, D), BF16),
+            pltpu.VMEM((chunks, 2 * HC * D, D), BF16),
+            pltpu.VMEM((2, chunks, HC * D, D), BF16),
             pltpu.SemaphoreType.DMA((3, chunks)),
             pltpu.SemaphoreType.DMA,
-            pltpu.SemaphoreType.DMA((STEPS, chunks)),
-            pltpu.SemaphoreType.DMA((STEPS, chunks)),
+            pltpu.SemaphoreType.DMA((UNIFORM + 4, chunks)),
+            pltpu.SemaphoreType.DMA((UNIFORM + 4, chunks)),
         ],
         compiler_params=pltpu.CompilerParams(
             collective_id=0, has_side_effects=True, vmem_limit_bytes=VL * 1024 * 1024

time: 51.1 us -> 46.7 us (0.914)
  the two profiles are of different devices: /device:TPU:0 before, /device:TPU:25 now
where the time goes in v3:
time: 46.7 us; the launch traced here: 46.6 us
  Pallas kernels  44.5 us (95%)
  local copies, waits for them, and re-layouts  2.02 us (4%)
    pallas_call x1, Pallas kernels, shards(): pl.pallas_call(functools.partial(kernel, heads), out_shape=pltpu.VMEM((ro...  44.5 us
    unnamed x1, local copies, waits for them, and re-layouts  2.02 us

profile of v3, /device:TPU:25, one launch (start us, length us, event | category | flops | bytes accessed | tf_op | source)
XLA Modules:
  0.0 46.6 jit_solution(2731552744082051984)
XLA Ops:
  0.0 44.5 %fenwick.1 = bf16[1024,2048]{1,0:T(8,128)(2,1)S(1)} custom-call(bf16[1024,2048]{1,0:T(8,128)(2,1)} %q_hbm.1, bf16[1024,2048]{1,0:T(8,128)(2,1)} %k_hbm.1, bf16[1024,2048]{1,0:T(8,128)(2,1)} %v_hbm.1, bf16[192,1024]{1,0:T(8,128)(2,1)} %bitcast.1), custom_call_target="tpu_custom_call" | custom-call | tf_op jit(solution)/shard_map/fenwick/pallas_call | solution.py:310
  44.5 2.0 %copy.6 = bf16[1024,2048]{1,0:T(8,128)(2,1)} copy(bf16[1024,2048]{1,0:T(8,128)(2,1)S(1)} %fenwick.1) | data formatting | bytes 8388608

commit v4 on v3

--- a/solution.py
+++ b/solution.py
@@ -260,8 +260,8 @@
 
     @pl.loop(0, chunks)
     def _(c):
+        states(c)
         exchanges(c)
-        states(c)
 
         @pl.when(c == GS)
         def _():

time: 46.7 us -> 46.6 us (level)
  no operation moved by 1% of the time
where the time goes in v4:
time: 46.6 us; the launch traced here: 46.5 us
  Pallas kernels  44.5 us (95%)
  local copies, waits for them, and re-layouts  2.02 us (4%)
    pallas_call x1, Pallas kernels, shards(): pl.pallas_call(functools.partial(kernel, heads), out_shape=pltpu.VMEM((ro...  44.5 us
    unnamed x1, local copies, waits for them, and re-layouts  2.02 us

profile of v4, /device:TPU:25, one launch (start us, length us, event | category | flops | bytes accessed | tf_op | source)
XLA Modules:
  0.0 46.5 jit_solution(5491304022786718766)
XLA Ops:
  0.0 44.5 %fenwick.1 = bf16[1024,2048]{1,0:T(8,128)(2,1)S(1)} custom-call(bf16[1024,2048]{1,0:T(8,128)(2,1)} %q_hbm.1, bf16[1024,2048]{1,0:T(8,128)(2,1)} %k_hbm.1, bf16[1024,2048]{1,0:T(8,128)(2,1)} %v_hbm.1, bf16[192,1024]{1,0:T(8,128)(2,1)} %bitcast.1), custom_call_target="tpu_custom_call" | custom-call | tf_op jit(solution)/shard_map/fenwick/pallas_call | solution.py:310
  44.5 2.0 %copy.6 = bf16[1024,2048]{1,0:T(8,128)(2,1)} copy(bf16[1024,2048]{1,0:T(8,128)(2,1)S(1)} %fenwick.1) | data formatting | bytes 8388608
